TPU v7x, 32 devices: a whole 2x2x4 slice. The times are simulated.
32 devices in a mesh: chan: 8 (over y, x, core), pulse: 4 (over z).
Axes of the slice: x: 2, y: 2, z: 4, core: 2. Of those that a mesh axis runs over, the one named last changes fastest.
Arguments:
- echoes: float32 [8, 2, 4096, 4096], P('chan', None, 'pulse'), may hold values from -6 to 6
- chirp_phase: float32 [4096], replicated, may hold values from -3.140625 to 3.140625
- rcmc_kernel: float32 [32, 128, 128], P('pulse'), may hold values from -0.5 to 0.5
- rcmc_offset: int32 [32], P('pulse'), may hold values from 1 to 64, as said below
- az_phase: float32 [4096, 32], P(None, 'pulse'), may hold values from -3.140625 to 3.140625
- weight_table: float32 [2, 64], replicated, may hold values from -1.5 to 1.5
- weight_index: int32 [8, 32], P('chan'), may hold values from 0 to 63
Outputs:
- image: float32 [2, 4096, 4096], P(None, 'chan', 'pulse')
Inputs may be any that keep to these rules, and one draw needn't show every extreme that they name: `rcmc_offset`: every offset is at least 1, and in every draw some block's offset equals 64.
All inputs are finite; a program needn't handle non-finite values.
Results may differ from a plain program's by a relative error of at most 0.0001.
Values sent between devices are 32-bit elements; how exact they have to be, the bound alone decides.
A program may use at most 256 MiB of HBM per device.

v0:
```python
import math

import jax
import jax.numpy as jnp
from jax import lax
from jax.sharding import PartitionSpec as P

BLOCK = 128
DBLOCK = 128
HALF = 64


def shifted(block, axis, distance):
    devices = range(lax.axis_size(axis))
    route = [(i - distance, i) for i in devices if i - distance in devices]
    return lax.ppermute(block, axis, route)


def factor_pair(length):
    return (128, length // 128)


def unit_table(count_a, count_b, modulus, sign_value):
    row_index = lax.broadcasted_iota(jnp.int32, (count_a, count_b), 0)
    col_index = lax.broadcasted_iota(jnp.int32, (count_a, count_b), 1)
    angles = (
        sign_value * 2.0 * math.pi / modulus * (row_index * col_index % modulus).astype(jnp.float32)
    )
    return (jnp.cos(angles), jnp.sin(angles))


def realify(coef_re, coef_im):
    return jnp.stack([jnp.stack([coef_re, coef_im]), jnp.stack([-coef_im, coef_re])])


def transform(stacked, sign_value, along_rows, prefactor=None):
    exact = lax.Precision.HIGHEST
    length = stacked.shape[1] if along_rows else stacked.shape[2]
    inner_len, outer_len = factor_pair(length)
    outer_re, outer_im = unit_table(outer_len, outer_len, outer_len, sign_value)
    inner_re, inner_im = unit_table(inner_len, inner_len, inner_len, sign_value)
    twist_re, twist_im = unit_table(outer_len, inner_len, length, sign_value)
    first_re = (
        outer_re[:, :, None] * twist_re[None, :, :] - outer_im[:, :, None] * twist_im[None, :, :]
    )
    first_im = (
        outer_re[:, :, None] * twist_im[None, :, :] + outer_im[:, :, None] * twist_re[None, :, :]
    )
    if prefactor is not None:
        pre_re = jnp.cos(prefactor).reshape(outer_len, inner_len)[:, None, :]
        pre_im = jnp.sin(prefactor).reshape(outer_len, inner_len)[:, None, :]
        first_re, first_im = (
            first_re * pre_re - first_im * pre_im,
            first_re * pre_im + first_im * pre_re,
        )
    first_table = realify(first_re, first_im)
    norm_scale = 1.0 / math.sqrt(length)
    second_table = realify(inner_re * norm_scale, inner_im * norm_scale)
    if along_rows:
        col_count = stacked.shape[2]
        data = stacked.reshape(2, outer_len, inner_len, col_count)
        middle = jnp.einsum("sabc,stakb->tkbc", data, first_table, precision=exact)
        result = jnp.einsum("tkbc,tubj->ujkc", middle, second_table, precision=exact)
        return result.reshape(2, length, col_count)
    row_count = stacked.shape[1]
    data = stacked.reshape(2, row_count, outer_len, inner_len)
    middle = jnp.einsum("srab,stakb->trkb", data, first_table, precision=exact)
    result = jnp.einsum("trkb,tubj->urjk", middle, second_table, precision=exact)
    return result.reshape(2, row_count, length)


def azimuth(exchanged):
    return transform(exchanged[:, :, 0, :], -1.0, True)[:, :, None, :]


def body(echoes, chirp_phase, rcmc_kernel, rcmc_offset, az_phase, weight_table, weight_index):
    own_data = echoes[0]
    pulses_dev = own_data.shape[1]
    gate_count = own_data.shape[2]
    pulse_devs = lax.axis_size("pulse")
    gates_dev = gate_count // pulse_devs
    spectrum = transform(own_data, -1.0, False)
    compressed = transform(spectrum, 1.0, False, chirp_phase)
    pieces = compressed.reshape(2, pulses_dev, pulse_devs, gates_dev)
    doppler = azimuth(lax.all_to_all(pieces, "pulse", split_axis=2, concat_axis=1, tiled=True))[
        :, :, 0, :
    ]
    beyond = shifted(doppler[:, :, :HALF], "pulse", -1)
    extended = jnp.concatenate([doppler, beyond], axis=2)
    pulses = extended.shape[1]
    rows_ext = extended.shape[2]
    blocks_dev = gates_dev // BLOCK
    row_ids = lax.broadcasted_iota(jnp.int32, (rows_ext, blocks_dev, BLOCK), 0)
    blk_ids = lax.broadcasted_iota(jnp.int32, (rows_ext, blocks_dev, BLOCK), 1)
    lane_ids = lax.broadcasted_iota(jnp.int32, (rows_ext, blocks_dev, BLOCK), 2)
    targets = blk_ids * BLOCK + rcmc_offset[None, :, None] + lane_ids
    selector = (row_ids == targets).astype(jnp.float32)
    banded = jnp.einsum("rbj,bjm->rbm", selector, rcmc_kernel, precision=lax.Precision.HIGHEST)
    banded = banded.reshape(rows_ext, gates_dev)
    migrated = jnp.einsum("cpr,rg->cpg", extended, banded, precision=lax.Precision.HIGHEST)
    table_count = weight_table.shape[1]
    entry_ids = lax.broadcasted_iota(jnp.int32, (weight_index.shape[1], table_count), 1)
    one_hot = (weight_index[0][:, None] == entry_ids).astype(jnp.float32)
    chosen = jnp.dot(one_hot, weight_table.T, precision=lax.Precision.HIGHEST)
    per_pulse = jnp.repeat(chosen, DBLOCK, axis=0)
    phase_re = jnp.cos(az_phase)
    phase_im = jnp.sin(az_phase)
    gain_re = (phase_re * per_pulse[:, 0:1] - phase_im * per_pulse[:, 1:2])[:, :, None]
    gain_im = (phase_re * per_pulse[:, 1:2] + phase_im * per_pulse[:, 0:1])[:, :, None]
    mig_re = migrated[0].reshape(pulses, blocks_dev, BLOCK)
    mig_im = migrated[1].reshape(pulses, blocks_dev, BLOCK)
    filt_re = (mig_re * gain_re - mig_im * gain_im).reshape(pulses, gates_dev)
    filt_im = (mig_re * gain_im + mig_im * gain_re).reshape(pulses, gates_dev)
    filtered = jnp.stack([filt_re, filt_im])
    shares = lax.psum_scatter(filtered, "chan", scatter_dimension=2, tiled=True)
    focused = transform(shares, 1.0, True)
    return lax.all_to_all(focused, "chan", split_axis=1, concat_axis=2, tiled=True)


def solution(mesh):
    return jax.shard_map(
        body,
        mesh=mesh,
        in_specs=(
            P("chan", None, "pulse", None),
            P(),
            P("pulse", None, None),
            P("pulse"),
            P(None, "pulse"),
            P(),
            P("chan", None),
        ),
        out_specs=P(None, "chan", "pulse"),
        check_vma=False,
    )
```

profile of v0, /device:TPU:0, one launch (start us, length us, event | category | flops | bytes accessed | tf_op | source)
XLA Modules:
  0.0 1959.2 jit_solution(10429190881014389413)
XLA Ops:
  21.3 7.6 copy.93
  28.9 17.2 copy.140
  46.2 11.3 bitcast_bitcast_fusion
  57.4 32.3 %copy.111 = f32[2,1024,32,128,1]{1,2,0,4,3:T(8,128)} copy(f32[2,1024,32,128,1]{3,2,1,0,4:T(8,128)} %bitcast_bitcast_fusion) | data formatting | bytes 67108864 | tf_op jit(solution)/shard_map/reshape;squeeze | solution.py:66
  89.8 38.8 %convolution_bitcast_fusion = f32[2,1024,32,128]{1,2,0,3:T(8,128)} fusion(f32[2,2,32,32,128]{2,3,0,1,4:T(8,128)} %copy.93, f32[2,1024,32,128,1]{1,2,0,4,3:T(8,128)} %copy.111), kind=kOutput, calls=%fused_computation.24 | convolution fusion | flops 6442450944 | bytes 69206016 | tf_op jit(solution)/shard_map/srab,stakb->trkb/dot_general | solution.py:67
  128.5 32.0 %copy.84 = f32[2,1024,32,128]{3,1,0,2:T(8,128)} copy(f32[2,1024,32,128]{1,2,0,3:T(8,128)} %convolution_bitcast_fusion) | data formatting | bytes 67108864 | tf_op jit(solution)/shard_map/srab,stakb->trkb/transpose | solution.py:67
  160.5 36.7 %fusion.15 = f32[2,1024,128,32]{1,2,3,0:T(8,128)} fusion(f32[2,1024,32,128]{3,1,0,2:T(8,128)} %copy.84, f32[1,2,128,128]{2,3,0,1:T(8,128)S(1)} %get-tuple-element.23, f32[1,2,128,128]{2,3,0,1:T(8,128)S(1)} %get-tuple-element.22), kind=kOutput, calls=%fused_computation.17 | convolution fusion | flops 25769869312 | bytes 67371008 | tf_op jit(solution)/shard_map/trkb,tubj->urjk/dot_general | solution.py:68
  197.2 31.8 %copy.85 = f32[2,1024,128,32]{1,3,2,0:T(8,128)} copy(f32[2,1024,128,32]{1,2,3,0:T(8,128)} %fusion.15) | data formatting | bytes 67108864 | tf_op jit(solution)/shard_map/trkb,tubj->urjk/transpose | solution.py:68
  229.0 62.2 %fusion.24 = f32[2,1024,32,128]{1,2,0,3:T(8,128)} fusion(f32[2,2,32,32,128]{2,3,0,1,4:T(8,128)} %copy.86, f32[2,1024,32,128,1]{1,3,2,0,4:T(8,128)} %bitcast.149), kind=kOutput, calls=%fused_computation.22 | convolution fusion | flops 6442450944 | bytes 69206016 | tf_op jit(solution)/shard_map/srab,stakb->trkb/dot_general | solution.py:67
  291.3 32.0 %copy.89 = f32[2,1024,32,128]{3,1,0,2:T(8,128)} copy(f32[2,1024,32,128]{1,2,0,3:T(8,128)} %fusion.24) | data formatting | bytes 67108864 | tf_op jit(solution)/shard_map/srab,stakb->trkb/transpose | solution.py:67
  324.1 36.5 %fusion.18 = f32[2,1024,128,32]{1,2,3,0:T(8,128)} fusion(f32[2,1024,32,128]{3,1,0,2:T(8,128)} %copy.89, f32[1,2,128,128]{2,3,1,0:T(8,128)S(1)} %get-tuple-element.21, f32[1,2,128,128]{2,3,1,0:T(8,128)S(1)} %get-tuple-element.20), kind=kOutput, calls=%fused_computation.18 | convolution fusion | flops 25769869312 | bytes 67371008 | tf_op jit(solution)/shard_map/trkb,tubj->urjk/dot_general | solution.py:68
  360.6 28.3 %copy.90 = f32[2,1024,128,32]{1,3,2,0:T(8,128)S(1)} copy(f32[2,1024,128,32]{1,2,3,0:T(8,128)} %fusion.18) | data formatting | bytes 67108864 | tf_op jit(solution)/shard_map/trkb,tubj->urjk/transpose | solution.py:68
  388.9 11.1 copy.91
  399.9 9.9 all-to-all-start
  410.3 723.6 %all-to-all-done = f32[2,1024,4,1024]{1,3,0,2:T(8,128)} async-done(((f32[2,1024,4,1024]{1,3,0,2:T(8,128)}), f32[2,1024,4,1024]{1,3,0,2:T(8,128)}, u32[]{:S(2)}, u32[]{:S(2)}) %all-to-all-start) | async-done | bytes 33554464 | tf_op jit(solution)/shard_map/all_to_all | solution.py:85
  1133.9 31.9 %copy.92 = f32[2,1024,4,1024]{3,1,2,0:T(8,128)} copy(f32[2,1024,4,1024]{1,3,0,2:T(8,128)} %all-to-all-done) | data formatting | bytes 67108864 | tf_op jit(solution)/shard_map/all_to_all | solution.py:85
  1165.8 62.2 %fusion.27 = f32[2,32,128,1024]{3,1,0,2:T(8,128)} fusion(f32[2,2,32,32,128]{2,3,0,1,4:T(8,128)} %copy.93, f32[2,32,128,1024,1]{3,2,1,0,4:T(8,128)} %bitcast.150), kind=kOutput, calls=%fused_computation.23 | convolution fusion | flops 6442450944 | bytes 69206016 | tf_op jit(solution)/shard_map/sabc,stakb->tkbc/dot_general | solution.py:62
  1228.1 70.9 %fusion.21 = f32[2,128,32,1024]{3,1,2,0:T(8,128)S(1)} fusion(f32[2,32,128,1024]{3,1,0,2:T(8,128)} %fusion.27, f32[1,2,128,128]{2,3,0,1:T(8,128)S(1)} %copy-done.8, f32[1,2,128,128]{2,3,0,1:T(8,128)S(1)} %copy-done.6), kind=kOutput, calls=%fused_computation.19 | convolution fusion | flops 25769869312 | bytes 67371008 | tf_op jit(solution)/shard_map/tkbc,tubj->ujkc/dot_general | solution.py:63
  1299.0 37.1 %copy.96 = f32[2,128,32,1024]{3,2,1,0:T(8,128)} copy(f32[2,128,32,1024]{3,1,2,0:T(8,128)S(1)} %fusion.21) | data formatting | bytes 67108864 | tf_op jit(solution)/shard_map/tkbc,tubj->ujkc/dot_general | solution.py:63
  1336.2 31.5 %copy.98 = f32[2,4096,1024]{1,2,0:T(8,128)} copy(f32[2,4096,1024]{2,1,0:T(8,128)} %bitcast.152) | data formatting | bytes 67108864 | tf_op jit(solution)/shard_map/squeeze;broadcast_in_dim;reshape | solution.py:85
  1388.2 10.7 mul.887
  1398.9 18.0 mul.888
  1417.5 10.7 mul.892
  1428.2 18.0 mul.893
  1446.3 140.6 %fusion = f32[2,4096,1024]{2,1,0:T(8,128)} fusion(f32[1088,1024,1]{1,0,2:T(8,128)} %reshape.279, f32[2,4096,64]{1,2,0:T(8,128)} %collective-permute-done, f32[2,4096,1024]{1,2,0:T(8,128)} %copy.98), kind=kOutput, calls=%fused_computation | convolution fusion | flops 109530578944 | bytes 73662464 | tf_op jit(solution)/shard_map/cpr,rg->cpg/dot_general | solution.py:100
  1586.8 34.0 %multiply_subtract_fusion = (f32[1,4096,1024]{2,1,0:T(8,128)}, f32[1,4096,1024]{2,1,0:T(8,128)}) fusion(f32[1,4096,1024]{2,1,0:T(8,128)} %mul.893, f32[1,4096,1024]{2,1,0:T(8,128)} %mul.888, f32[2,4096,1024]{2,1,0:T(8,128)} %fusion), kind=kLoop, calls=%fused_computation.21 | loop fusion | flops 25165824 | bytes 100663296 | tf_op jit(solution)/shard_map/sub | solution.py:112
  1620.8 23.5 %pad_maximum_fusion = f32[2,4096,1024]{2,1,0:T(8,128)} fusion(f32[1,4096,1024]{2,1,0:T(8,128)} %get-tuple-element.6, f32[1,4096,1024]{2,1,0:T(8,128)} %get-tuple-element.5), kind=kLoop, calls=%fused_computation.5 | loop fusion | flops 8388608 | bytes 67108864 | tf_op jit(solution)/shard_map/stack | solution.py:114
  1646.1 7.6 copy.122
  1653.6 196.7 %reduce-scatter.2.cloned.1.call-done = f32[2,4096,128]{2,1,0:T(8,128)} async-done(((f32[2,4096,1024]{2,1,0:T(8,128)}), f32[2,4096,128]{2,1,0:T(8,128)}) %reduce-scatter.2.cloned.1.call-update) | async-done | bytes 4194320 | tf_op jit(solution)/shard_map/reduce_scatter | solution.py:115
  1850.3 13.2 fusion.41
  1871.9 15.6 copy.107
  1887.6 51.6 %all_to_all.33 = f32[2,4096,128]{2,0,1:T(2,128)S(1)} all-to-all(f32[2,4096,128]{2,0,1:T(2,128)S(1)} %copy.107), channel_id=1, replica_groups=mesh['chan'=8,'pulse'=4] {'chan'}, dimensions={1} | all-to-all | bytes 8388608 | tf_op jit(solution)/shard_map/all_to_all | solution.py:117
  (75 shorter events, 60.1 us)
Async XLA Ops:
  6.5 1365.6 %copy-start = (f32[8,128,128]{2,1,0:T(8,128)S(1)}, f32[8,128,128]{2,1,0:T(8,128)}, u32[]{:S(2)}) copy-start(f32[8,128,128]{2,1,0:T(8,128)} %param.9) | copy-start | bytes 1572868
  160.5 36.7 %copy-start.5 = (f32[1,2,128,128]{2,3,0,1:T(8,128)}, f32[1,2,128,128]{2,3,0,1:T(8,128)S(1)}, u32[]{:S(2)}) copy-start(f32[1,2,128,128]{2,3,0,1:T(8,128)S(1)} %get-tuple-element.22) | copy-start | bytes 393220
  160.5 36.7 %copy-start.7 = (f32[1,2,128,128]{2,3,0,1:T(8,128)}, f32[1,2,128,128]{2,3,0,1:T(8,128)S(1)}, u32[]{:S(2)}) copy-start(f32[1,2,128,128]{2,3,0,1:T(8,128)S(1)} %get-tuple-element.23) | copy-start | bytes 393220
  291.3 32.1 %copy-start.9 = (f32[1,128,128]{1,2,0:T(8,128)S(1)}, f32[1,128,128]{1,2,0:T(8,128)}, u32[]{:S(2)}) copy-start(f32[1,128,128]{1,2,0:T(8,128)} %get-tuple-element.42) | copy-start | bytes 196612
  291.3 32.1 %copy-start.10 = (f32[1,128,128]{1,2,0:T(8,128)S(1)}, f32[1,128,128]{1,2,0:T(8,128)}, u32[]{:S(2)}) copy-start(f32[1,128,128]{1,2,0:T(8,128)} %get-tuple-element.43) | copy-start | bytes 196612
  291.3 32.1 %copy-start.11 = (f32[1,128,128]{1,2,0:T(8,128)S(1)}, f32[1,128,128]{1,2,0:T(8,128)}, u32[]{:S(2)}) copy-start(f32[1,128,128]{1,2,0:T(8,128)} %fusion.53) | copy-start | bytes 196612
  323.4 0.7 copy-start.1
  323.4 0.7 copy-start.3
  399.9 9.9 copy-start.13
  399.9 9.9 copy-start.14
  399.9 10.3 copy-start.15
  399.9 734.0 %all-to-all-start = ((f32[2,1024,4,1024]{1,3,0,2:T(8,128)}), f32[2,1024,4,1024]{1,3,0,2:T(8,128)}, u32[]{:S(2)}, u32[]{:S(2)}) async-start(f32[2,1024,4,1024]{1,3,0,2:T(8,128)} %copy.91), calls=%async_computation | async-start | bytes 67108864 | tf_op jit(solution)/shard_map/all_to_all | solution.py:85
  409.8 1440.5 %reduce-scatter.2.cloned.1.call-start = ((), (), s32[]{:S(2)}) async-start(), calls=%async_computation.3 | async-start | bytes 37748736 | tf_op jit(solution)/shard_map/reduce_scatter | solution.py:115
  1165.8 62.3 %copy-start.6 = (f32[1,2,128,128]{2,3,0,1:T(8,128)S(1)}, f32[1,2,128,128]{2,3,0,1:T(8,128)}, u32[]{:S(2)}) copy-start(f32[1,2,128,128]{2,3,0,1:T(8,128)} %copy-done.5) | copy-start | bytes 393220
  1165.8 62.3 %copy-start.8 = (f32[1,2,128,128]{2,3,0,1:T(8,128)S(1)}, f32[1,2,128,128]{2,3,0,1:T(8,128)}, u32[]{:S(2)}) copy-start(f32[1,2,128,128]{2,3,0,1:T(8,128)} %copy-done.7) | copy-start | bytes 393220
  1367.7 19.4 copy-start.12
  1370.8 75.5 %collective-permute-start = (f32[2,4096,64]{1,2,0:T(8,128)}, f32[2,4096,64]{1,2,0:T(8,128)}, u32[]{:S(2)}, u32[]{:S(2)}) collective-permute-start(f32[2,4096,64]{1,2,0:T(8,128)} %slice.22), channel_id=1, source_target_pairs={{1,0},{2,1},{3,2},{5,4},{6,5},{7,6},{9,8},{10,9},{11,10},{13,12},{... | collective-permute-start | bytes 6291464 | tf_op jit(solution)/shard_map/ppermute | solution.py:16
  1644.3 219.3 %copy-start.2 = (f32[1,2,128,128]{2,3,1,0:T(8,128)S(1)}, f32[1,2,128,128]{2,3,1,0:T(8,128)}, u32[]{:S(2)}) copy-start(f32[1,2,128,128]{2,3,1,0:T(8,128)} %copy-done.1) | copy-start | bytes 393220
  1644.3 219.3 %copy-start.4 = (f32[1,2,128,128]{2,3,1,0:T(8,128)S(1)}, f32[1,2,128,128]{2,3,1,0:T(8,128)}, u32[]{:S(2)}) copy-start(f32[1,2,128,128]{2,3,1,0:T(8,128)} %copy-done.3) | copy-start | bytes 393220
Sparse Core Ops, SparseCore 0:
  1644.4 205.8 reduce-scatter.1
where the time goes:
time: 1970 us; the launch traced here: 1960 us
  waiting for transfers between devices  920 us (47%)
  matrix products  469 us (24%)
  local copies, waits for them, and re-layouts  427 us (22%)
  other arithmetic  65.7 us (3%)
  blocking collectives  51.6 us (3%)
    all_to_all x1, waiting for transfers between devices, body(): lax.all_to_all(pieces, 'pulse', split_axis=2, concat_axis=1, tiled=True)  724 us
    reduce_scatter x1, waiting for transfers between devices, body(): shares = lax.psum_scatter(filtered, 'chan', scatter_dimension=2, tiled=True)  197 us
    dot_general x1, matrix products, body(): jnp.einsum('cpr,rg->cpg', extended, banded, precision=lax.Precision.HIGHEST)  141 us
    dot_general x2, matrix products, transform(): middle = jnp.einsum('srab,stakb->trkb', data, first_table, precision=exact)  101 us
    dot_general x2, matrix products, transform(): jnp.einsum('tkbc,tubj->ujkc', middle, second_table, precision=exact)  76.8 us
    dot_general x2, matrix products, transform(): middle = jnp.einsum('sabc,stakb->tkbc', data, first_table, precision=exact)  75.5 us
    dot_general x2, matrix products, transform(): jnp.einsum('trkb,tubj->urjk', middle, second_table, precision=exact)  73.1 us
    transpose x2, local copies, waits for them, and re-layouts, transform(): middle = jnp.einsum('srab,stakb->trkb', data, first_table, precision=exact)  64 us
  transfers between devices with their start and end apart: 3, of which 2 were waited for; matrix products, arithmetic and copies ran while one was open for 4% of the time, Pallas kernels for 0%

commit v1 on v0

v1 whole, which is shorter than its diff:
```python
import math

import jax
import jax.numpy as jnp
from jax import lax
from jax.sharding import PartitionSpec as P

BLOCK = 128
CHUNKS = 4
PRECISION = lax.Precision.HIGH


def factor_pair(length):
    return (128, length // 128)


def unit_table(count_a, count_b, modulus, sign_value, start_a=0):
    row_index = lax.broadcasted_iota(jnp.int32, (count_a, count_b), 0) + start_a
    col_index = lax.broadcasted_iota(jnp.int32, (count_a, count_b), 1)
    angles = (
        sign_value * 2.0 * math.pi / modulus * (row_index * col_index % modulus).astype(jnp.float32)
    )
    return (jnp.cos(angles), jnp.sin(angles))


def realify(coef_re, coef_im):
    return jnp.stack([jnp.stack([coef_re, coef_im]), jnp.stack([-coef_im, coef_re])])


def transform(stacked, sign_value, along_rows, prefactor=None):
    length = stacked.shape[1] if along_rows else stacked.shape[2]
    inner_len, outer_len = factor_pair(length)
    outer_re, outer_im = unit_table(outer_len, outer_len, outer_len, sign_value)
    inner_re, inner_im = unit_table(inner_len, inner_len, inner_len, sign_value)
    twist_re, twist_im = unit_table(outer_len, inner_len, length, sign_value)
    first_re = (
        outer_re[:, :, None] * twist_re[None, :, :] - outer_im[:, :, None] * twist_im[None, :, :]
    )
    first_im = (
        outer_re[:, :, None] * twist_im[None, :, :] + outer_im[:, :, None] * twist_re[None, :, :]
    )
    if prefactor is not None:
        pre_re = jnp.cos(prefactor).reshape(outer_len, inner_len)[:, None, :]
        pre_im = jnp.sin(prefactor).reshape(outer_len, inner_len)[:, None, :]
        first_re, first_im = (
            first_re * pre_re - first_im * pre_im,
            first_re * pre_im + first_im * pre_re,
        )
    first_table = realify(first_re, first_im)
    norm_scale = 1.0 / math.sqrt(length)
    second_table = realify(inner_re * norm_scale, inner_im * norm_scale)
    if along_rows:
        col_count = stacked.shape[2]
        data = stacked.reshape(2, outer_len, inner_len, col_count)
        middle = jnp.einsum("sabc,stakb->tkbc", data, first_table, precision=PRECISION)
        result = jnp.einsum("tkbc,tubj->ujkc", middle, second_table, precision=PRECISION)
        return result.reshape(2, length, col_count)
    row_count = stacked.shape[1]
    data = stacked.reshape(2, row_count, outer_len, inner_len)
    middle = jnp.einsum("srab,stakb->trkb", data, first_table, precision=PRECISION)
    result = jnp.einsum("trkb,tubj->urjk", middle, second_table, precision=PRECISION)
    return result.reshape(2, row_count, length)


def body(echoes, chirp_phase, rcmc_kernel, rcmc_offset, az_phase, weight_table, weight_index):
    own = echoes[0]
    pulses_dev, gates = own.shape[1], own.shape[2]
    chans = lax.axis_size("chan")
    pulse_devs = lax.axis_size("pulse")
    pulses = pulses_dev * pulse_devs
    dblocks = weight_index.shape[1]
    bins = pulses // dblocks
    coarse = pulses_dev // dblocks
    z = lax.axis_index("pulse")
    j = lax.axis_index("chan")

    kernels = lax.all_gather(rcmc_kernel, "pulse", axis=0, tiled=True)
    offsets = lax.all_gather(rcmc_offset, "pulse", axis=0, tiled=True)
    phases = lax.all_gather(az_phase, "pulse", axis=1, tiled=True)
    indices = lax.all_gather(weight_index[0], "chan", axis=0, tiled=False)

    fine_re, fine_im = unit_table(pulses_dev, bins, pulses, -1.0, z * pulses_dev)
    fine = realify(fine_re, fine_im).reshape(2, 2, coarse, dblocks, bins)
    entry_ids = lax.broadcasted_iota(jnp.int32, (chans, dblocks, weight_table.shape[1]), 2)
    one_hot = (indices[:, :, None] == entry_ids).astype(jnp.float32)
    chosen = jnp.einsum("cen,wn->wce", one_hot, weight_table, precision=lax.Precision.HIGHEST)
    step_re, step_im = unit_table(dblocks, dblocks, dblocks, -1.0)
    norm_scale = 1.0 / math.sqrt(pulses)
    w_re, w_im = chosen[0][:, None, :] * norm_scale, chosen[1][:, None, :] * norm_scale
    mix = realify(step_re * w_re - step_im * w_im, step_re * w_im + step_im * w_re)

    width = gates // CHUNKS
    parts = []
    for chunk in range(CHUNKS):
        piece = own[:, :, chunk * width : (chunk + 1) * width]
        piece = piece.reshape(2, pulses_dev, chans, width // chans)
        piece = jnp.transpose(piece, (2, 0, 1, 3))
        held = lax.all_to_all(piece, "chan", split_axis=0, concat_axis=0, tiled=True)
        held = held.reshape(chans, 2, coarse, dblocks, width // chans)
        middle = jnp.einsum("csabg,stabr->bctrg", held, fine, precision=PRECISION)
        summed = jnp.einsum("bctrg,tucbe->uerg", middle, mix, precision=PRECISION)
        summed = summed.reshape(2, pulses, width // chans)
        parts.append(lax.psum_scatter(summed, "pulse", scatter_dimension=1, tiled=True))

    joined = jnp.stack(parts)
    rows = joined.shape[2] // chans
    joined = joined.reshape(CHUNKS, 2, chans, rows, width // chans)
    joined = jnp.transpose(joined, (2, 0, 1, 3, 4))
    joined = lax.all_to_all(joined, "chan", split_axis=0, concat_axis=0, tiled=True)
    doppler = jnp.transpose(joined, (2, 3, 1, 0, 4)).reshape(2, rows, gates)

    spectrum = transform(doppler, -1.0, False)
    compressed = transform(spectrum, 1.0, False, chirp_phase)
    blocks = gates // BLOCK
    split = compressed.reshape(2, rows, blocks, BLOCK)
    after = jnp.pad(split[:, :, 1:], ((0, 0), (0, 0), (0, 1), (0, 0)))
    window = jnp.concatenate([split, after], axis=3)
    at = lax.broadcasted_iota(jnp.int32, (blocks, 2 * BLOCK, BLOCK), 1)
    lane = lax.broadcasted_iota(jnp.int32, (blocks, 2 * BLOCK, BLOCK), 2)
    selector = (at == offsets[:, None, None] + lane).astype(jnp.float32)
    banded = jnp.einsum("brj,bjm->brm", selector, kernels, precision=lax.Precision.HIGHEST)
    migrated = jnp.einsum("sdbr,brm->sdbm", window, banded, precision=PRECISION)

    angle = lax.dynamic_slice_in_dim(phases, (z * chans + j) * rows, rows, axis=0)
    cos, sin = jnp.cos(angle)[:, :, None], jnp.sin(angle)[:, :, None]
    filtered = jnp.stack(
        [migrated[0] * cos - migrated[1] * sin, migrated[0] * sin + migrated[1] * cos]
    ).reshape(2, rows, gates)

    shares = lax.all_to_all(filtered, ("pulse", "chan"), split_axis=2, concat_axis=1, tiled=True)
    focused = transform(shares, 1.0, True)
    return lax.all_to_all(focused, "chan", split_axis=1, concat_axis=2, tiled=True)


def solution(mesh):
    return jax.shard_map(
        body,
        mesh=mesh,
        in_specs=(
            P("chan", None, "pulse", None),
            P(),
            P("pulse", None, None),
            P("pulse"),
            P(None, "pulse"),
            P(),
            P("chan", None),
        ),
        out_specs=P(None, "chan", "pulse"),
        check_vma=False,
    )
```

time: 1970 us -> 995 us (0.51)
  waiting for transfers between devices: 920 us -> 167 us
  local copies, waits for them, and re-layouts: 427 us -> 248 us
  matrix products: 469 us -> 336 us
  blocking collectives: 51.6 us -> 172 us
  other arithmetic: 65.7 us -> 19.7 us
    all_to_all x1 -> x6, waiting for transfers between devices: 724 us -> 91.9 us  [the longest x1 84.7 us: body(): lax.all_to_all(filtered, ('pulse', 'chan'), split_axis=2, concat_axis=1,...]
    dot_general x11 -> x17, matrix products: 469 us -> 336 us  [the longest x4 176 us: body(): summed = jnp.einsum('bctrg,tucbe->uerg', middle, mix, precision=PRECISION)]
    reduce_scatter x1 -> x4, waiting for transfers between devices: 197 us -> 71.1 us  [body(): lax.psum_scatter(summed, 'pulse', scatter_dimension=1, tiled=True)]
    all_gather x0 -> x2, blocking collectives: none -> 111 us  [the longest x1 89 us: body(): indices = lax.all_gather(weight_index[0], 'chan', axis=0, tiled=False)]
    transpose x5 -> x8, local copies, waits for them, and re-layouts: 131 us -> 46.5 us  [the longest x4 29.1 us: body(): piece = jnp.transpose(piece, (2, 0, 1, 3))]
    mul x4 -> x0, local copies, waits for them, and re-layouts: 57.4 us -> none  [body(): filt_re = (mig_re * gain_re - mig_im * gain_im).reshape(pulses, gates_dev)]
    another operation x2 -> x1, local copies, waits for them, and re-layouts: 43.6 us -> 6.08 us  [transform(): data = stacked.reshape(2, row_count, outer_len, inner_len)]
    sub x1, other arithmetic: 34 us -> 0.7 us  [body(): migrated[0] * cos - migrated[1] * sin]
  transfers between devices with their start and end apart: 3 -> 11, of which waited for: 2 -> 4; matrix products, arithmetic and copies ran while one was open for 4% -> 42% of each run, Pallas kernels for 0% -> 0%
where the time goes in v1:
time: 995 us; the launch traced here: 987 us
  matrix products  336 us (34%)
  local copies, waits for them, and re-layouts  248 us (25%)
  blocking collectives  172 us (17%)
  waiting for transfers between devices  167 us (17%)
  starting transfers between devices  29 us (3%)
  other arithmetic  19.7 us (2%)
  between operations  14.5 us (1%)
    dot_general x4, matrix products, body(): summed = jnp.einsum('bctrg,tucbe->uerg', middle, mix, precision=PRECISION)  176 us
    dot_general x4, matrix products, body(): middle = jnp.einsum('csabg,stabr->bctrg', held, fine, precision=PRECISION)  107 us
    all_gather x1, blocking collectives, body(): indices = lax.all_gather(weight_index[0], 'chan', axis=0, tiled=False)  89 us
    all_to_all x1, waiting for transfers between devices, body(): lax.all_to_all(filtered, ('pulse', 'chan'), split_axis=2, concat_axis=1,...  84.7 us
    reduce_scatter x4, waiting for transfers between devices, body(): lax.psum_scatter(summed, 'pulse', scatter_dimension=1, tiled=True)  71.1 us
    all_to_all x1, blocking collectives, body(): lax.all_to_all(focused, 'chan', split_axis=1, concat_axis=2, tiled=True)  52.6 us
    all_to_all x4, local copies, waits for them, and re-layouts, body(): lax.all_to_all(piece, 'chan', split_axis=0, concat_axis=0, tiled=True)  36.8 us
    unnamed x30, local copies, waits for them, and re-layouts  32.1 us
  transfers between devices with their start and end apart: 11, of which 4 were waited for; matrix products, arithmetic and copies ran while one was open for 42% of the time, Pallas kernels for 0%

profile of v1, /device:TPU:0, one launch (start us, length us, event | category | flops | bytes accessed | tf_op | source)
XLA Modules:
  0.0 986.9 jit_solution(1240710565739295214)
XLA Ops:
  6.5 31.2 %copy.160 = f32[1,2,1024,4096]{2,3,1,0:T(8,128)} copy(f32[1,2,1024,4096]{3,2,1,0:T(8,128)} %param.7) | data formatting | bytes 67108864 | tf_op args[0]
  37.7 22.3 %fusion.118 = (f32[2,1024,1024]{1,2,0:T(8,128)S(1)}, f32[2,1024,1024]{1,2,0:T(8,128)}, f32[2,1024,1024]{1,2,0:T(8,128)}, f32[2,1024,1024]{1,2,0:T(8,128)}) fusion(f32[2,1024,4096]{1,2,0:T(8,128)} %bitcast.250), kind=kLoop, calls=%fused_computation.167 | loop fusion | bytes 67108864 | tf_op jit(solution)/shard_map/slice | solution.py:95
  69.3 8.3 copy.166
  77.6 89.0 %all-gather = s32[8,1,32]{2,1,0:T(1,128)S(1)} all-gather(s32[1,1,32]{2,1,0:T(1,128)S(1)} %bitcast.279), channel_id=1, replica_groups=mesh['chan'=8,'pulse'=4] {'chan'}, dimensions={0}, use_global_device_ids=true | all-gather | bytes 1152 | tf_op jit(solution)/shard_map/all_gather | solution.py:80
  175.1 9.2 copy.162
  184.2 26.7 %convolution_bitcast_fusion.3 = f32[32,8,2,128,128]{4,3,1,2,0:T(8,128)} fusion(f32[8,2,32,32,128,1]{4,3,2,1,0,5:T(8,128)} %bitcast.252, f32[1,1,32,32,128]{4,2,0,1,3:T(8,128)S(1)} %get-tuple-element.39, f32[1,1,32,32,128]{4,2,0,1,3:T(8,128)S(1)} %get-tuple-element.38, f32[1,1,32,32,128]{4,2,0,1,3:T(8,128)S(1)} %get-tuple-element.37), kind=kOutput, calls=%fused_computation.15 | convolution fusion | flops 3222798336 | bytes 43515904 | tf_op jit(solution)/shard_map/csabg,stabr->bctrg/dot_general | solution.py:100
  210.9 44.1 %fusion.48 = f32[2,32,128,128]{3,1,2,0:T(8,128)} fusion(f32[32,8,2,128,128]{4,3,1,2,0:T(8,128)} %convolution_bitcast_fusion.3, f32[1,2,8,32,32]{3,4,0,2,1:T(8,128)S(1)} %get-tuple-element.20, f32[1,2,8,32,32]{3,4,0,2,1:T(8,128)S(1)} %get-tuple-element.19), kind=kOutput, calls=%fused_computation.49 | convolution fusion | flops 3221258240 | bytes 37879808 | tf_op jit(solution)/shard_map/bctrg,tucbe->uerg/dot_general | solution.py:101
  261.7 8.3 copy.171
  275.1 9.2 copy.167
  284.2 26.8 %convolution_bitcast_fusion.2 = f32[32,8,2,128,128]{4,3,1,2,0:T(8,128)} fusion(f32[8,2,32,32,128,1]{4,3,2,1,0,5:T(8,128)} %bitcast.253, f32[1,1,32,32,128]{4,2,0,1,3:T(8,128)S(1)} %get-tuple-element.39, f32[1,1,32,32,128]{4,2,0,1,3:T(8,128)S(1)} %get-tuple-element.38, f32[1,1,32,32,128]{4,2,0,1,3:T(8,128)S(1)} %get-tuple-element.37), kind=kOutput, calls=%fused_computation.14 | convolution fusion | flops 3222798336 | bytes 43515904 | tf_op jit(solution)/shard_map/csabg,stabr->bctrg/dot_general | solution.py:100
  311.0 44.1 %fusion.51 = f32[2,32,128,128]{3,1,2,0:T(8,128)} fusion(f32[32,8,2,128,128]{4,3,1,2,0:T(8,128)} %convolution_bitcast_fusion.2, f32[1,2,8,32,32]{3,4,0,2,1:T(8,128)S(1)} %get-tuple-element.20, f32[1,2,8,32,32]{3,4,0,2,1:T(8,128)S(1)} %get-tuple-element.19), kind=kOutput, calls=%fused_computation.50 | convolution fusion | flops 3221258240 | bytes 37879808 | tf_op jit(solution)/shard_map/bctrg,tucbe->uerg/dot_general | solution.py:101
  361.7 8.3 copy.176
  375.1 9.2 copy.172
  384.3 26.8 %convolution_bitcast_fusion.1 = f32[32,8,2,128,128]{4,3,1,2,0:T(8,128)} fusion(f32[8,2,32,32,128,1]{4,3,2,1,0,5:T(8,128)} %bitcast.254, f32[1,1,32,32,128]{4,2,0,1,3:T(8,128)S(1)} %get-tuple-element.39, f32[1,1,32,32,128]{4,2,0,1,3:T(8,128)S(1)} %get-tuple-element.38, f32[1,1,32,32,128]{4,2,0,1,3:T(8,128)S(1)} %get-tuple-element.37), kind=kOutput, calls=%fused_computation.13 | convolution fusion | flops 3222798336 | bytes 43515904 | tf_op jit(solution)/shard_map/csabg,stabr->bctrg/dot_general | solution.py:100
  411.0 44.1 %fusion.54 = f32[2,32,128,128]{3,1,2,0:T(8,128)} fusion(f32[32,8,2,128,128]{4,3,1,2,0:T(8,128)} %convolution_bitcast_fusion.1, f32[1,2,8,32,32]{3,4,0,2,1:T(8,128)S(1)} %get-tuple-element.20, f32[1,2,8,32,32]{3,4,0,2,1:T(8,128)S(1)} %get-tuple-element.19), kind=kOutput, calls=%fused_computation.51 | convolution fusion | flops 3221258240 | bytes 37879808 | tf_op jit(solution)/shard_map/bctrg,tucbe->uerg/dot_general | solution.py:101
  461.8 7.2 all-to-all-done.3
  469.1 9.3 copy.177
  478.4 26.7 %convolution_bitcast_fusion = f32[32,8,2,128,128]{4,3,1,2,0:T(8,128)} fusion(f32[8,2,32,32,128,1]{4,3,2,1,0,5:T(8,128)} %bitcast.251, f32[1,1,32,32,128]{4,2,0,1,3:T(8,128)S(1)} %get-tuple-element.39, f32[1,1,32,32,128]{4,2,0,1,3:T(8,128)S(1)} %get-tuple-element.38, f32[1,1,32,32,128]{4,2,0,1,3:T(8,128)S(1)} %get-tuple-element.37), kind=kOutput, calls=%fused_computation.12 | convolution fusion | flops 3222798336 | bytes 43515904 | tf_op jit(solution)/shard_map/csabg,stabr->bctrg/dot_general | solution.py:100
  505.1 43.9 %fusion.57 = f32[2,32,128,128]{3,1,2,0:T(8,128)} fusion(f32[32,8,2,128,128]{4,3,1,2,0:T(8,128)} %convolution_bitcast_fusion, f32[1,2,8,32,32]{3,4,0,2,1:T(8,128)S(1)} %get-tuple-element.20, f32[1,2,8,32,32]{3,4,0,2,1:T(8,128)S(1)} %get-tuple-element.19), kind=kOutput, calls=%fused_computation.52 | convolution fusion | flops 3221258240 | bytes 37879808 | tf_op jit(solution)/shard_map/bctrg,tucbe->uerg/dot_general | solution.py:101
  562.6 71.0 %reduce-scatter.11.cloned.1.call-done = f32[2,1024,128]{2,1,0:T(8,128)} async-done(((f32[2,4096,128]{2,1,0:T(8,128)}), f32[2,1024,128]{2,1,0:T(8,128)}) %reduce-scatter.11.cloned.1.call-update) | async-done | bytes 1048592 | tf_op jit(solution)/shard_map/reduce_scatter | solution.py:103
  647.8 8.0 copy.186
  658.7 7.6 copy.190
  667.9 9.2 all-reduce.1
  677.1 21.6 %all_gather.15 = f32[4096,32]{0,1:T(8,128)S(1)} all-gather(f32[4096,8]{0,1:T(8,128)S(1)} %copy-done.6), channel_id=1, replica_groups=mesh['chan'=8,'pulse'=4] {'pulse'}, dimensions={1}, use_global_device_ids=true | all-gather | bytes 655360 | tf_op jit(solution)/shard_map/all_gather | solution.py:79
  715.7 10.0 %fusion.66 = f32[2,128,32,128]{1,2,0,3:T(8,128)} fusion(f32[2,2,32,32,128]{2,3,0,1,4:T(8,128)} %copy.186, f32[8,4,2,128,128]{3,0,1,2,4:T(8,128)} %copy.251), kind=kOutput, calls=%fused_computation.55 | convolution fusion | flops 402653184 | bytes 10485760 | tf_op jit(solution)/shard_map/srab,stakb->trkb/dot_general | solution.py:60
  737.3 8.8 fusion.63
  767.7 7.8 fusion.45
  786.3 7.6 copy.233
  793.9 84.7 %all-to-all-done.5 = f32[2,128,4096]{1,0,2:T(2,128)} async-done(((f32[2,128,4096]{1,0,2:T(2,128)}), f32[2,128,4096]{1,0,2:T(2,128)}, u32[]{:S(2)}, u32[]{:S(2)}) %all-to-all-start.5) | async-done | bytes 4194336 | tf_op jit(solution)/shard_map/all_to_all | solution.py:130
  884.0 8.3 fusion.60
  899.0 15.6 %copy.205 = f32[2,4096,128]{2,0,1:T(2,128)S(1)} copy(f32[2,4096,128]{2,1,0:T(8,128)S(1)} %bitcast.266) | data formatting | bytes 8388608 | tf_op jit(solution)/shard_map/reshape | solution.py:57
  914.7 52.6 %all_to_all.58 = f32[2,4096,128]{2,0,1:T(2,128)S(1)} all-to-all(f32[2,4096,128]{2,0,1:T(2,128)S(1)} %copy.205), channel_id=1, replica_groups=mesh['chan'=8,'pulse'=4] {'chan'}, dimensions={1} | all-to-all | bytes 8388608 | tf_op jit(solution)/shard_map/all_to_all | solution.py:132
  (114 shorter events, 164.9 us)
Async XLA Ops:
  6.5 160.2 %copy-start = (f32[2,64]{1,0:T(2,128)S(1)}, f32[2,64]{1,0:T(2,128)}, u32[]{:S(2)}) copy-start(f32[2,64]{1,0:T(2,128)} %param.12) | copy-start | bytes 1540
  64.1 105.5 %all-to-all-start = ((f32[8,2,1024,128]{2,3,1,0:T(8,128)}), f32[8,2,1024,128]{2,3,1,0:T(8,128)}, u32[]{:S(2)}, u32[]{:S(2)}) async-start(f32[8,2,1024,128]{2,3,1,0:T(8,128)} %copy.161), calls=%async_computation | async-start | bytes 16777216 | tf_op jit(solution)/shard_map/all_to_all | solution.py:98
  69.3 8.3 copy-start.8
  166.7 0.6 copy-start.2
  166.7 0.6 copy-start.4
  169.6 100.5 %all-to-all-start.1 = ((f32[8,2,1024,128]{2,3,1,0:T(8,128)}), f32[8,2,1024,128]{2,3,1,0:T(8,128)}, u32[]{:S(2)}, u32[]{:S(2)}) async-start(f32[8,2,1024,128]{2,3,1,0:T(8,128)} %copy.166), calls=%async_computation.2 | async-start | bytes 16777216 | tf_op jit(solution)/shard_map/all_to_all | solution.py:98
  174.6 381.1 %reduce-scatter.5.cloned.1.call-start = ((), (), s32[]{:S(2)}) async-start(), calls=%async_computation.12 | async-start | bytes 5242880 | tf_op jit(solution)/shard_map/reduce_scatter | solution.py:103
  270.0 100.0 %all-to-all-start.2 = ((f32[8,2,1024,128]{2,3,1,0:T(8,128)}), f32[8,2,1024,128]{2,3,1,0:T(8,128)}, u32[]{:S(2)}, u32[]{:S(2)}) async-start(f32[8,2,1024,128]{2,3,1,0:T(8,128)} %copy.171), calls=%async_computation.4 | async-start | bytes 16777216 | tf_op jit(solution)/shard_map/all_to_all | solution.py:98
  275.0 283.0 %reduce-scatter.7.cloned.1.call-start = ((), (), s32[]{:S(2)}) async-start(), calls=%async_computation.13 | async-start | bytes 5242880 | tf_op jit(solution)/shard_map/reduce_scatter | solution.py:103
  370.0 99.0 %all-to-all-start.3 = ((f32[8,2,1024,128]{2,3,1,0:T(8,128)}), f32[8,2,1024,128]{2,3,1,0:T(8,128)}, u32[]{:S(2)}, u32[]{:S(2)}) async-start(f32[8,2,1024,128]{2,3,1,0:T(8,128)} %copy.176), calls=%async_computation.6 | async-start | bytes 16777216 | tf_op jit(solution)/shard_map/all_to_all | solution.py:98
  375.0 185.3 %reduce-scatter.9.cloned.1.call-start = ((), (), s32[]{:S(2)}) async-start(), calls=%async_computation.14 | async-start | bytes 5242880 | tf_op jit(solution)/shard_map/reduce_scatter | solution.py:103
  461.8 171.9 %reduce-scatter.11.cloned.1.call-start = ((), (), s32[]{:S(2)}) async-start(), calls=%async_computation.15 | async-start | bytes 5242880 | tf_op jit(solution)/shard_map/reduce_scatter | solution.py:103
  641.4 5.3 copy-start.5
  641.4 5.4 copy-start.3
  641.4 68.1 %all-to-all-start.4 = ((f32[8,4,2,128,128]{4,1,3,2,0:T(4,128)}), f32[8,4,2,128,128]{4,1,3,2,0:T(4,128)}, u32[]{:S(2)}, u32[]{:S(2)}) async-start(f32[8,4,2,128,128]{4,1,3,2,0:T(4,128)} %maximum_bitcast_fusion), calls=%async_computation.8 | async-start | bytes 8388608 | tf_op jit(solution)/shard_map/all_to_all | solution.py:109
  646.1 57.4 %all-gather.3.cloned.1.call-start = ((), (), s32[]{:S(2)}) async-start(), calls=%async_computation.11 | async-start | bytes 2621440 | tf_op jit(solution)/shard_map/all_gather | solution.py:77
  647.8 8.5 copy-start.7
  658.7 7.7 copy-start.10
  658.7 8.9 copy-start.9
  658.7 18.4 %copy-start.6 = (f32[4096,8]{0,1:T(8,128)S(1)}, f32[4096,8]{0,1:T(8,128)}, u32[]{:S(2)}) copy-start(f32[4096,8]{0,1:T(8,128)} %param.11) | copy-start | bytes 393220
  731.0 6.3 slice-start.1
  731.0 6.3 slice-start.2
  765.6 2.2 slice-start
  781.1 97.5 %all-to-all-start.5 = ((f32[2,128,4096]{1,0,2:T(2,128)}), f32[2,128,4096]{1,0,2:T(2,128)}, u32[]{:S(2)}, u32[]{:S(2)}) async-start(f32[2,128,4096]{1,0,2:T(2,128)} %pad_maximum_fusion), calls=%async_computation.9 | async-start | bytes 8388608 | tf_op jit(solution)/shard_map/all_to_all | solution.py:130
  974.9 5.4 copy-start.1
Sparse Core Ops, SparseCore 0:
  261.8 79.1 reduce-scatter.4
  361.9 79.4 reduce-scatter.6
  461.9 79.6 reduce-scatter.8
  555.7 77.8 reduce-scatter.10
  648.2 55.2 all-gather.2
